TPU v7x, 32 devices: a whole 2x2x4 slice. The times are simulated.
32 devices in a mesh: grp: 2 (over y), kin: 4 (over z), nout: 4 (over x, core).
Axes of the slice: x: 2, y: 2, z: 4, core: 2. Of those that a mesh axis runs over, the one named last changes fastest.
Arguments:
- normed: bfloat16 [64, 14848], P(('grp', 'nout'), 'kin'), parts along dimension 0, may hold values from -6 to 6
- keep_masks: int32 [16, 14848], P('grp', 'kin'), parts along dimension 0, may hold values 0 or 1
- qkv_weight: bfloat16 [14848, 15872], P('kin', 'nout'), may hold values from -0.046875 to 0.046875
- up_weight: bfloat16 [14848, 29696], P('kin', 'nout'), may hold values from -0.046875 to 0.046875
Outputs:
- qkv_out: bfloat16 [64, 8, 15872], P(('grp', 'kin'), None, 'nout'), parts along dimension 0
- hidden_out: bfloat16 [64, 8, 29696], P(('grp', 'kin'), None, 'nout'), parts along dimension 0
There are 2 independent parts, one for each index of `grp`. A program takes and returns all parts, laid end to end along the dimension named above; an argument that names none is the same for every part. Nothing has to cross between parts.
All inputs are finite; a program needn't handle non-finite values. No bound on the sum of `keep_masks` on one device may be relied on, other than what follows from the above.
Results may differ from a plain program's by a relative error of at most 0.013.
Values may be sent and summed in bfloat16 or wider, within the bound.
A program may use at most 192 MiB of HBM per device.

v0:
```python
import jax
import jax.numpy as jnp
from jax import lax
from jax.sharding import PartitionSpec as P

KEEP_SCALE = 10.0 / 9.0


def local(normed, keep_masks, qkv_weight, up_weight):
    gathered = lax.all_gather(normed, "nout", axis=0, tiled=True)
    all_tokens = gathered.shape[0]
    passes = keep_masks.shape[0]
    width = gathered.shape[1]
    qkv_cols = qkv_weight.shape[1]
    up_cols = up_weight.shape[1]
    dropped = (
        gathered.astype(jnp.float32)[:, None, :]
        * keep_masks.astype(jnp.float32)[None, :, :]
        * KEEP_SCALE
    )
    dropped = dropped.astype(jnp.bfloat16)
    own_tokens = all_tokens // lax.axis_size("kin")
    rows = dropped.reshape(own_tokens * lax.axis_size("kin") * passes, width)
    first = jnp.dot(rows, qkv_weight, preferred_element_type=jnp.float32)
    second = jnp.dot(rows, up_weight, preferred_element_type=jnp.float32)
    joined = jnp.concatenate([first, second], axis=1)
    summed = lax.psum_scatter(
        joined.reshape(own_tokens * lax.axis_size("kin"), passes, qkv_cols + up_cols).astype(
            jnp.bfloat16
        ),
        "kin",
        scatter_dimension=0,
        tiled=True,
    ).astype(jnp.float32)
    qkv_out = summed[:, :, :qkv_cols].astype(jnp.bfloat16)
    hidden_out = jax.nn.gelu(summed[:, :, qkv_cols:], approximate=False).astype(jnp.bfloat16)
    return (qkv_out, hidden_out)


def solution(mesh):
    placed = (P(("grp", "nout"), "kin"), P("grp", "kin"), P("kin", "nout"), P("kin", "nout"))
    return jax.shard_map(
        local,
        mesh=mesh,
        in_specs=placed,
        out_specs=(P(("grp", "kin"), None, "nout"), P(("grp", "kin"), None, "nout")),
        check_vma=False,
    )
```

profile of v0, /device:TPU:0, one launch (start us, length us, event | category | flops | bytes accessed | tf_op | source)
XLA Modules:
  0.0 178.2 jit_solution(17873309365237776376)
XLA Ops:
  7.2 0.0 reduce-scatter.2.cloned.1.call-start
  7.2 0.9 convert_element_type.23
  8.1 7.3 %all_gather.3 = bf16[32,3712]{1,0:T(8,128)(2,1)S(1)} all-gather(bf16[8,3712]{1,0:T(8,128)(2,1)} %param.4), channel_id=1, replica_groups=mesh['grp'=2,'kin'=4,'nout'=4] {'nout'}, dimensions={0}, use_global_device_ids=true | all-gather | bytes 296960 | tf_op jit(solution)/shard_map/all_gather | solution.py:10
  15.4 13.5 %convolution_convert_fusion.1 = bf16[256,3968]{1,0:T(8,128)(2,1)S(1)} fusion(bf16[3712,3968]{1,0:T(8,128)(2,1)} %param.6, f32[8,3712]{1,0:T(8,128)S(1)} %convert_element_type.23, f32[32,3712]{1,0:T(8,128)S(1)} %convert_element_type.22), kind=kOutput, calls=%fused_computation.2 | convolution fusion | flops 7545225216 | bytes 32083968 | tf_op jit(solution)/shard_map/dot_general | solution.py:24
  28.9 24.8 %convolution_convert_fusion = bf16[256,7424]{1,0:T(8,128)(2,1)} fusion(bf16[3712,7424]{1,0:T(8,128)(2,1)} %param.7, f32[8,3712]{1,0:T(8,128)S(1)} %convert_element_type.23, f32[32,3712]{1,0:T(8,128)S(1)} %convert_element_type.22), kind=kOutput, calls=%fused_computation | convolution fusion | flops 14114390016 | bytes 59510784 | tf_op jit(solution)/shard_map/dot_general | solution.py:25
  53.8 5.0 %maximum_bitcast_fusion = bf16[32,8,11392]{2,1,0:T(8,128)(2,1)} fusion(bf16[256,7424]{1,0:T(8,128)(2,1)} %convolution_convert_fusion, bf16[256,3968]{1,0:T(8,128)(2,1)S(1)} %convolution_convert_fusion.1), kind=kLoop, calls=%fused_computation.1 | loop fusion | flops 11665408 | bytes 11665408 | tf_op jit(solution)/shard_map/convert_element_type | solution.py:28
  58.7 0.0 reduce-scatter.2.cloned.1.call-update
  58.8 104.9 %reduce-scatter.2.cloned.1.call-done = bf16[8,8,11392]{2,1,0:T(8,128)(2,1)} async-done(((bf16[32,8,11392]{2,1,0:T(8,128)(2,1)}), bf16[8,8,11392]{2,1,0:T(8,128)(2,1)}) %reduce-scatter.2.cloned.1.call-update) | async-done | bytes 1458192 | tf_op jit(solution)/shard_map/reduce_scatter | solution.py:27
  163.6 1.9 %slice.13 = bf16[8,8,3968]{2,1,0:T(8,128)(2,1)} slice(bf16[8,8,11392]{2,1,0:T(8,128)(2,1)} %reduce-scatter.2.cloned.1.call-done), slice={[0:8], [0:8], [0:3968]} | slice | bytes 1015808 | tf_op jit(solution)/shard_map/slice | solution.py:35
  165.5 5.9 %fusion.1 = bf16[8,8,7424]{2,1,0:T(8,128)(2,1)} fusion(bf16[8,8,11392]{2,1,0:T(8,128)(2,1)} %reduce-scatter.2.cloned.1.call-done), kind=kLoop, calls=%fused_computation.8 | loop fusion | flops 31358976 | bytes 1900544 | tf_op jit(solution)/shard_map/convert_element_type | solution.py:36
  (1 shorter events, 0.0 us)
Async XLA Ops:
  7.2 156.5 %reduce-scatter.2.cloned.1.call-start = ((), (), s32[]{:S(2)}) async-start(), calls=%async_computation.1 | async-start | bytes 7290880 | tf_op jit(solution)/shard_map/reduce_scatter | solution.py:27
Sparse Core Ops, SparseCore 0:
  58.9 104.6 reduce-scatter.1
where the time goes:
time: 179 us; the launch traced here: 178 us
  waiting for transfers between devices  105 us (59%)
  matrix products  38.3 us (21%)
  between operations  14 us (8%)
  other arithmetic  11.8 us (7%)
  blocking collectives  7.27 us (4%)
  local copies, waits for them, and re-layouts  1.85 us (1%)
    reduce_scatter x1, waiting for transfers between devices, local(): lax.psum_scatter(joined.reshape(own_tokens * lax.axis_size('kin'), passes...  105 us
    dot_general x1, matrix products, local(): second = jnp.dot(rows, up_weight, preferred_element_type=jnp.float32)  24.8 us
    dot_general x1, matrix products, local(): first = jnp.dot(rows, qkv_weight, preferred_element_type=jnp.float32)  13.5 us
    all_gather x1, blocking collectives, local(): gathered = lax.all_gather(normed, 'nout', axis=0, tiled=True)  7.27 us
    convert_element_type x1, other arithmetic, local(): jax.nn.gelu(summed[:, :, qkv_cols:], approximate=False).astype(jnp.bfloat16)  5.89 us
    convert_element_type x1, other arithmetic, local(): joined.reshape(own_tokens * lax.axis_size('kin'), passes, qkv_cols + up_c...  4.97 us
  transfers between devices with their start and end apart: 1, of which 1 were waited for; matrix products, arithmetic and copies ran while one was open for 0% of the time, Pallas kernels for 0%

commit v1 on v0

v1 whole, which is shorter than its diff:
```python
import functools

import jax
import jax.numpy as jnp
from jax import lax
from jax.experimental import pallas as pl
from jax.experimental.pallas import tpu as pltpu
from jax.sharding import PartitionSpec as P

KEEP_SCALE = 10.0 / 9.0
WIDE = 256
SLOTS = 3
LAG = 3
MESH = pl.DeviceIdType.MESH


def gelu(v):
    return v * (1.0 + lax.erf(v * (0.5**0.5))) * 0.5


def kernel(
    n, peers, passes, head, nq, chunks,
    normed_ref, mask_ref, qkv_ref, up_ref, qkv_out, up_out,
    gathered, dropped, tiles, own, rising, falling,
    gather_send, gather_recv, tile_sem, send_sem, rise_recv, fall_recv,
):
    z = lax.axis_index("kin")
    mine = lax.axis_index("nout")
    above = jnp.minimum(z + 1, n - 1)
    below = jnp.maximum(z - 1, 0)
    block = own.shape[2]

    def tile_copy(c, slot):
        def go(act):
            @pl.when(c < nq)
            def _():
                col = pl.multiple_of(head + (c - 1) * WIDE, 128)
                act(pltpu.make_async_copy(qkv_ref.at[:, pl.ds(col, WIDE)], tiles.at[slot], tile_sem.at[slot]))

            @pl.when(c >= nq)
            def _():
                col = pl.multiple_of((c - nq) * WIDE, 128)
                act(pltpu.make_async_copy(up_ref.at[:, pl.ds(col, WIDE)], tiles.at[slot], tile_sem.at[slot]))
        return go

    first_tile = pltpu.make_async_copy(qkv_ref.at[:, pl.ds(0, head)], tiles.at[0, :, pl.ds(0, head)], tile_sem.at[0])
    first_tile.start()
    for c in range(1, min(SLOTS, chunks)):
        tile_copy(c, c)(lambda copy: copy.start())

    barrier = pltpu.get_barrier_semaphore()
    for k in range(1, peers):
        pl.semaphore_signal(barrier, inc=1, device_id={"nout": lax.rem(mine + k, peers)}, device_id_type=MESH)

    @pl.when(z < n - 1)
    def _():
        pl.semaphore_signal(barrier, inc=1, device_id={"kin": above}, device_id_type=MESH)

    @pl.when(z > 0)
    def _():
        pl.semaphore_signal(barrier, inc=1, device_id={"kin": below}, device_id_type=MESH)

    pl.semaphore_wait(barrier, peers - 1 + jnp.where(z < n - 1, 1, 0) + jnp.where(z > 0, 1, 0))

    def gather_copy(k):
        return pltpu.make_async_remote_copy(
            src_ref=normed_ref, dst_ref=gathered.at[k - 1],
            send_sem=gather_send.at[k - 1], recv_sem=gather_recv.at[k - 1],
            device_id={"nout": lax.rem(mine + k, peers)}, device_id_type=MESH,
        )

    for k in range(1, peers):
        gather_copy(k).start()

    keep = mask_ref[...].astype(jnp.float32)
    tokens = normed_ref.shape[0]

    def drop(x, source):
        x = x.astype(jnp.float32)
        for r in range(0, tokens, 2):
            pair = [x[t : t + 1, :] * keep * KEEP_SCALE for t in (r, r + 1)]
            row = pl.multiple_of((source * tokens + r) * passes, 2 * passes)
            dropped[pl.ds(row, 2 * passes), :] = jnp.concatenate(pair, axis=0).astype(jnp.bfloat16)

    drop(normed_ref[...], mine)
    for k in range(1, peers):
        gather_copy(k).wait_recv()
        drop(gathered[k - 1], lax.rem(mine - k + peers, peers))

    def sized(c, body):
        @pl.when(c == 0)
        def _():
            body(0, head)

        @pl.when((c > 0) & (c < chunks))
        def _():
            body(c, WIDE)

    def rise_copy(c, d, width):
        part = (c, d, slice(None), pl.ds(0, width))
        return pltpu.make_async_remote_copy(
            src_ref=rising.at[part], dst_ref=rising.at[part],
            send_sem=send_sem.at[c, d], recv_sem=rise_recv.at[c, d],
            device_id={"kin": above}, device_id_type=MESH,
        )

    def fall_copy(c, d, width):
        part = (c, d, slice(None), pl.ds(0, width))
        return pltpu.make_async_remote_copy(
            src_ref=falling.at[part], dst_ref=falling.at[part],
            send_sem=send_sem.at[c, d], recv_sem=fall_recv.at[c, d],
            device_id={"kin": below}, device_id_type=MESH,
        )

    def compute(c, width):
        slot = lax.rem(c, SLOTS)
        if width == WIDE and not isinstance(c, int):
            tile_copy(c, slot)(lambda copy: copy.wait())
        else:
            first_tile.wait()
        got = jnp.dot(dropped[...], tiles[slot, :, :width], preferred_element_type=jnp.float32)
        own[c, :, :, :width] = got.reshape(n, block, width)

        @pl.when(c + SLOTS < chunks)
        def _():
            tile_copy(c + SLOTS, slot)(lambda copy: copy.start())

    def forward(buffer, copy_of, at_end, count, target):
        def body(c, width):
            def one(i, carry):
                d = target(i)

                @pl.when(at_end)
                def _():
                    buffer[c, d, :, :width] = own[c, d, :, :width].astype(jnp.bfloat16)

                @pl.when(jnp.logical_not(at_end))
                def _():
                    copy_of(c, d, width).wait_recv()
                    buffer[c, d, :, :width] = (
                        buffer[c, d, :, :width].astype(jnp.float32) + own[c, d, :, :width]
                    ).astype(jnp.bfloat16)

                copy_of(c, d, width).start()
                return carry

            lax.fori_loop(0, count, one, 0)
        return body

    rise = forward(rising, rise_copy, z == 0, n - 1 - z, lambda i: n - 1 - i)
    fall = forward(falling, fall_copy, z == n - 1, z, lambda i: i)

    def finish(c, width):
        @pl.when(z > 0)
        def _():
            rise_copy(c, z, width).wait_recv()
            own[c, z, :, :width] += rising[c, z, :, :width].astype(jnp.float32)

        @pl.when(z < n - 1)
        def _():
            fall_copy(c, z, width).wait_recv()
            own[c, z, :, :width] += falling[c, z, :, :width].astype(jnp.float32)

        total = own[c, z, :, :width]
        if isinstance(c, int):
            qkv_out[:, :width] = total.astype(jnp.bfloat16)
        else:
            @pl.when(c < nq)
            def _():
                col = pl.multiple_of(head + (c - 1) * WIDE, 128)
                qkv_out[:, pl.ds(col, WIDE)] = total.astype(jnp.bfloat16)

            @pl.when(c >= nq)
            def _():
                col = pl.multiple_of((c - nq) * WIDE, 128)
                up_out[:, pl.ds(col, WIDE)] = gelu(total).astype(jnp.bfloat16)

    def step(s, carry):
        sized(s, compute)
        sized(s - LAG * z, rise)
        sized(s - LAG * (n - 1 - z), fall)
        sized(s - LAG * (n - 1), finish)
        return carry

    lax.fori_loop(0, chunks + LAG * (n - 1), step, 0)

    for k in range(1, peers):
        gather_copy(k).wait_send()

    def drain(c, width):
        def up(i, carry):
            rise_copy(c, n - 1 - i, width).wait_send()
            return carry

        def down(i, carry):
            fall_copy(c, i, width).wait_send()
            return carry

        lax.fori_loop(0, n - 1 - z, up, 0)
        lax.fori_loop(0, z, down, 0)

    def drain_step(c, carry):
        sized(c, drain)
        return carry

    lax.fori_loop(0, chunks, drain_step, 0)


def fused(normed, keep_masks, qkv_weight, up_weight):
    n, peers = lax.axis_size("kin"), lax.axis_size("nout")
    tokens, width = normed.shape
    passes = keep_masks.shape[0]
    qkv_cols, up_cols = qkv_weight.shape[1], up_weight.shape[1]
    head = qkv_cols % WIDE or WIDE
    nq = 1 + (qkv_cols - head) // WIDE
    chunks = nq + up_cols // WIDE
    rows = tokens * peers * passes
    block = rows // n
    vmem = pl.BlockSpec(memory_space=pltpu.VMEM)
    hbm = pl.BlockSpec(memory_space=pl.ANY)
    qkv_out, up_out = pl.pallas_call(
        functools.partial(kernel, n, peers, passes, head, nq, chunks),
        out_shape=(
            jax.ShapeDtypeStruct((block, qkv_cols), jnp.bfloat16),
            jax.ShapeDtypeStruct((block, up_cols), jnp.bfloat16),
        ),
        in_specs=[vmem, vmem, hbm, hbm],
        out_specs=(vmem, vmem),
        scratch_shapes=[
            pltpu.VMEM((peers - 1, tokens, width), jnp.bfloat16),
            pltpu.VMEM((rows, width), jnp.bfloat16),
            pltpu.VMEM((SLOTS, width, WIDE), jnp.bfloat16),
            pltpu.VMEM((chunks, n, block, WIDE), jnp.float32),
            pltpu.VMEM((chunks, n, block, WIDE), jnp.bfloat16),
            pltpu.VMEM((chunks, n, block, WIDE), jnp.bfloat16),
            pltpu.SemaphoreType.DMA((peers - 1,)),
            pltpu.SemaphoreType.DMA((peers - 1,)),
            pltpu.SemaphoreType.DMA((SLOTS,)),
            pltpu.SemaphoreType.DMA((chunks, n)),
            pltpu.SemaphoreType.DMA((chunks, n)),
            pltpu.SemaphoreType.DMA((chunks, n)),
        ],
        compiler_params=pltpu.CompilerParams(
            collective_id=0, has_side_effects=True, vmem_limit_bytes=52 * 2**20
        ),
        cost_estimate=pl.CostEstimate(
            flops=2 * rows * width * (qkv_cols + up_cols),
            bytes_accessed=2 * width * (qkv_cols + up_cols),
            transcendentals=block * up_cols,
        ),
    )(normed, keep_masks, qkv_weight, up_weight)
    own_tokens = block // passes
    return (
        qkv_out.reshape(own_tokens, passes, qkv_cols),
        up_out.reshape(own_tokens, passes, up_cols),
    )


def plain(normed, keep_masks, qkv_weight, up_weight):
    gathered = lax.all_gather(normed, "nout", axis=0, tiled=True)
    all_tokens, width = gathered.shape
    passes = keep_masks.shape[0]
    qkv_cols, up_cols = qkv_weight.shape[1], up_weight.shape[1]
    dropped = (
        gathered.astype(jnp.float32)[:, None, :]
        * keep_masks.astype(jnp.float32)[None, :, :]
        * KEEP_SCALE
    )
    rows = dropped.astype(jnp.bfloat16).reshape(all_tokens * passes, width)
    first = jnp.dot(rows, qkv_weight, preferred_element_type=jnp.float32)
    second = jnp.dot(rows, up_weight, preferred_element_type=jnp.float32)
    joined = jnp.concatenate([first, second], axis=1)
    summed = lax.psum_scatter(
        joined.reshape(all_tokens, passes, qkv_cols + up_cols).astype(jnp.bfloat16),
        "kin",
        scatter_dimension=0,
        tiled=True,
    ).astype(jnp.float32)
    qkv_out = summed[:, :, :qkv_cols].astype(jnp.bfloat16)
    hidden_out = jax.nn.gelu(summed[:, :, qkv_cols:], approximate=False).astype(jnp.bfloat16)
    return (qkv_out, hidden_out)


def local(normed, keep_masks, qkv_weight, up_weight):
    tokens, width = normed.shape
    passes = keep_masks.shape[0]
    n, peers = lax.axis_size("kin"), lax.axis_size("nout")
    aligned = (
        width % 128 == 0
        and qkv_weight.shape[1] % 128 == 0
        and up_weight.shape[1] % WIDE == 0
        and tokens % 2 == 0
        and passes == 8
        and (tokens * peers * passes // n) % 16 == 0
    )
    run = fused if aligned else plain
    return run(normed, keep_masks, qkv_weight, up_weight)


def solution(mesh):
    placed = (P(("grp", "nout"), "kin"), P("grp", "kin"), P("kin", "nout"), P("kin", "nout"))
    return jax.shard_map(
        local,
        mesh=mesh,
        in_specs=placed,
        out_specs=(P(("grp", "kin"), None, "nout"), P(("grp", "kin"), None, "nout")),
        check_vma=False,
    )
```

time: 179 us -> 121 us (0.68)
  Pallas kernels: 0 us -> 116 us
  waiting for transfers between devices: 105 us -> 0 us
  matrix products: 38.3 us -> 0 us
  between operations: 14 us -> 0.65 us
  other arithmetic: 11.8 us -> 0 us
  blocking collectives: 7.27 us -> 0 us
    pallas_call x0 -> x1, Pallas kernels: none -> 116 us  [fused(): pl.pallas_call(functools.partial(kernel, n, peers, passes, head, nq, chun...]
    reduce_scatter x1 -> x0, waiting for transfers between devices: 105 us -> none  [local(): lax.psum_scatter(joined.reshape(own_tokens * lax.axis_size('kin'), passes...]
    dot_general x2 -> x0, matrix products: 38.3 us -> none  [the longest x1 24.8 us: local(): second = jnp.dot(rows, up_weight, preferred_element_type=jnp.float32)]
    convert_element_type x4 -> x0, other arithmetic: 11.8 us -> none  [the longest x1 5.89 us: local(): jax.nn.gelu(summed[:, :, qkv_cols:], approximate=False).astype(jnp.bfloat16)]
    all_gather x1 -> x0, blocking collectives: 7.27 us -> none  [local(): gathered = lax.all_gather(normed, 'nout', axis=0, tiled=True)]
    unnamed x0 -> x6, local copies, waits for them, and re-layouts: none -> 3.44 us
    slice x1 -> x0, local copies, waits for them, and re-layouts: 1.85 us -> none  [local(): qkv_out = summed[:, :, :qkv_cols].astype(jnp.bfloat16)]
  transfers between devices with their start and end apart: 1 -> 0, of which waited for: 1 -> 0; matrix products, arithmetic and copies ran while one was open for 0% -> 0% of each run, Pallas kernels for 0% -> 0%
where the time goes in v1:
time: 121 us; the launch traced here: 120 us
  Pallas kernels  116 us (96%)
  local copies, waits for them, and re-layouts  3.44 us (3%)
    pallas_call x1, Pallas kernels, fused(): pl.pallas_call(functools.partial(kernel, n, peers, passes, head, nq, chun...  116 us
    unnamed x6, local copies, waits for them, and re-layouts  3.44 us

profile of v1, /device:TPU:0, one launch (start us, length us, event | category | flops | bytes accessed | tf_op | source)
XLA Modules:
  0.0 120.4 jit_solution(13858021924325208605)
XLA Ops:
  0.6 0.0 copy-start
  0.6 0.9 copy-done
  1.5 0.0 copy-start.1
  1.5 0.8 copy-done.1
  2.4 116.3 %shard_map.59 = (bf16[64,3968]{1,0:T(8,128)(2,1)S(1)}, bf16[64,7424]{1,0:T(8,128)(2,1)S(1)}) custom-call(bf16[8,3712]{1,0:T(8,128)(2,1)S(1)} %copy-done.1, s32[8,3712]{1,0:T(8,128)S(1)} %copy-done, bf16[3712,3968]{1,0:T(8,128)(2,1)} %qkv_ref.1, bf16[3712,7424]{1,0:T(8,128)(2,1)} %up_ref.1), custom_call_target="tpu_custom_call" | custom-call | flops 21650997248 | bytes 84574208 | tf_op jit(solution)/shard_map/pallas_call | solution.py:221
  118.7 0.8 copy.8
  119.4 0.9 copy.9
Async XLA Ops:
  0.6 0.9 copy-start
  1.5 0.8 copy-start.1

commit v2 on v1

--- a/solution.py
+++ b/solution.py
@@ -10,7 +10,7 @@
 KEEP_SCALE = 10.0 / 9.0
 WIDE = 256
 SLOTS = 3
-LAG = 3
+LAG = 4
 MESH = pl.DeviceIdType.MESH
 
 
@@ -21,8 +21,8 @@
 def kernel(
     n, peers, passes, head, nq, chunks,
     normed_ref, mask_ref, qkv_ref, up_ref, qkv_out, up_out,
-    gathered, dropped, tiles, own, rising, falling,
-    gather_send, gather_recv, tile_sem, send_sem, rise_recv, fall_recv,
+    gathered, mask, dropped, tiles, own, rising, falling,
+    own_sem, mask_sem, gather_send, gather_recv, tile_sem, send_sem, rise_recv, fall_recv,
 ):
     z = lax.axis_index("kin")
     mine = lax.axis_index("nout")
@@ -43,14 +43,24 @@
                 act(pltpu.make_async_copy(up_ref.at[:, pl.ds(col, WIDE)], tiles.at[slot], tile_sem.at[slot]))
         return go
 
+    own_copy = pltpu.make_async_copy(normed_ref, gathered.at[0], own_sem)
+    own_copy.start()
+    mask_copy = pltpu.make_async_copy(mask_ref, mask, mask_sem)
+    mask_copy.start()
     first_tile = pltpu.make_async_copy(qkv_ref.at[:, pl.ds(0, head)], tiles.at[0, :, pl.ds(0, head)], tile_sem.at[0])
     first_tile.start()
-    for c in range(1, min(SLOTS, chunks)):
-        tile_copy(c, c)(lambda copy: copy.start())
+    def peer(k):
+        at = mine
+        bit = 1
+        while bit < peers:
+            if k & bit:
+                at = at + bit - 2 * bit * ((mine // bit) % 2)
+            bit *= 2
+        return at
 
     barrier = pltpu.get_barrier_semaphore()
     for k in range(1, peers):
-        pl.semaphore_signal(barrier, inc=1, device_id={"nout": lax.rem(mine + k, peers)}, device_id_type=MESH)
+        pl.semaphore_signal(barrier, inc=1, device_id={"nout": peer(k)}, device_id_type=MESH)
 
     @pl.when(z < n - 1)
     def _():
@@ -64,15 +74,18 @@
 
     def gather_copy(k):
         return pltpu.make_async_remote_copy(
-            src_ref=normed_ref, dst_ref=gathered.at[k - 1],
+            src_ref=normed_ref, dst_ref=gathered.at[k],
             send_sem=gather_send.at[k - 1], recv_sem=gather_recv.at[k - 1],
-            device_id={"nout": lax.rem(mine + k, peers)}, device_id_type=MESH,
+            device_id={"nout": peer(k)}, device_id_type=MESH,
         )
 
-    for k in range(1, peers):
+    for k in range(peers - 1, 0, -1):
         gather_copy(k).start()
-
-    keep = mask_ref[...].astype(jnp.float32)
+    for c in range(1, min(SLOTS, chunks)):
+        tile_copy(c, c)(lambda copy: copy.start())
+
+    mask_copy.wait()
+    keep = mask[...].astype(jnp.float32)
     tokens = normed_ref.shape[0]
 
     def drop(x, source):
@@ -82,10 +95,11 @@
             row = pl.multiple_of((source * tokens + r) * passes, 2 * passes)
             dropped[pl.ds(row, 2 * passes), :] = jnp.concatenate(pair, axis=0).astype(jnp.bfloat16)
 
-    drop(normed_ref[...], mine)
+    own_copy.wait()
+    drop(gathered[0], mine)
     for k in range(1, peers):
         gather_copy(k).wait_recv()
-        drop(gathered[k - 1], lax.rem(mine - k + peers, peers))
+        drop(gathered[k], peer(k))
 
     def sized(c, body):
         @pl.when(c == 0)
@@ -125,30 +139,21 @@
         def _():
             tile_copy(c + SLOTS, slot)(lambda copy: copy.start())
 
-    def forward(buffer, copy_of, at_end, count, target):
+    def forward(buffer, copy_of, at_end, d):
         def body(c, width):
-            def one(i, carry):
-                d = target(i)
-
-                @pl.when(at_end)
-                def _():
-                    buffer[c, d, :, :width] = own[c, d, :, :width].astype(jnp.bfloat16)
-
-                @pl.when(jnp.logical_not(at_end))
-                def _():
-                    copy_of(c, d, width).wait_recv()
-                    buffer[c, d, :, :width] = (
-                        buffer[c, d, :, :width].astype(jnp.float32) + own[c, d, :, :width]
-                    ).astype(jnp.bfloat16)
-
-                copy_of(c, d, width).start()
-                return carry
-
-            lax.fori_loop(0, count, one, 0)
+            @pl.when(at_end)
+            def _():
+                buffer[c, d, :, :width] = own[c, d, :, :width].astype(jnp.bfloat16)
+
+            @pl.when(jnp.logical_not(at_end))
+            def _():
+                copy_of(c, d, width).wait_recv()
+                buffer[c, d, :, :width] = (
+                    buffer[c, d, :, :width].astype(jnp.float32) + own[c, d, :, :width]
+                ).astype(jnp.bfloat16)
+
+            copy_of(c, d, width).start()
         return body
-
-    rise = forward(rising, rise_copy, z == 0, n - 1 - z, lambda i: n - 1 - i)
-    fall = forward(falling, fall_copy, z == n - 1, z, lambda i: i)
 
     def finish(c, width):
         @pl.when(z > 0)
@@ -177,8 +182,18 @@
 
     def step(s, carry):
         sized(s, compute)
-        sized(s - LAG * z, rise)
-        sized(s - LAG * (n - 1 - z), fall)
+
+        def rise(i, carry):
+            d = n - 1 - i
+            sized(s - LAG * (z + i), forward(rising, rise_copy, z == 0, d))
+            return carry
+
+        def fall(d, carry):
+            sized(s - LAG * (n - 1 - z + d), forward(falling, fall_copy, z == n - 1, d))
+            return carry
+
+        lax.fori_loop(0, n - 1 - z, rise, 0)
+        lax.fori_loop(0, z, fall, 0)
         sized(s - LAG * (n - 1), finish)
         return carry
 
@@ -224,15 +239,18 @@
             jax.ShapeDtypeStruct((block, qkv_cols), jnp.bfloat16),
             jax.ShapeDtypeStruct((block, up_cols), jnp.bfloat16),
         ),
-        in_specs=[vmem, vmem, hbm, hbm],
+        in_specs=[hbm, hbm, hbm, hbm],
         out_specs=(vmem, vmem),
         scratch_shapes=[
-            pltpu.VMEM((peers - 1, tokens, width), jnp.bfloat16),
+            pltpu.VMEM((peers, tokens, width), jnp.bfloat16),
+            pltpu.VMEM((passes, width), jnp.int32),
             pltpu.VMEM((rows, width), jnp.bfloat16),
             pltpu.VMEM((SLOTS, width, WIDE), jnp.bfloat16),
             pltpu.VMEM((chunks, n, block, WIDE), jnp.float32),
             pltpu.VMEM((chunks, n, block, WIDE), jnp.bfloat16),
             pltpu.VMEM((chunks, n, block, WIDE), jnp.bfloat16),
+            pltpu.SemaphoreType.DMA,
+            pltpu.SemaphoreType.DMA,
             pltpu.SemaphoreType.DMA((peers - 1,)),
             pltpu.SemaphoreType.DMA((peers - 1,)),
             pltpu.SemaphoreType.DMA((SLOTS,)),
@@ -290,6 +308,7 @@
         and qkv_weight.shape[1] % 128 == 0
         and up_weight.shape[1] % WIDE == 0
         and tokens % 2 == 0
+        and peers & (peers - 1) == 0
         and passes == 8
         and (tokens * peers * passes // n) % 16 == 0
     )

time: 121 us -> 116 us (0.959)
  Pallas kernels: 116 us -> 112 us
    pallas_call x1, Pallas kernels: 116 us -> 112 us  [fused(): pl.pallas_call(functools.partial(kernel, n, peers, passes, head, nq, chun...]
where the time goes in v2:
time: 116 us
  Pallas kernels  112 us (97%)
  local copies, waits for them, and re-layouts  3.44 us (3%)
    pallas_call x1, Pallas kernels, fused(): pl.pallas_call(functools.partial(kernel, n, peers, passes, head, nq, chun...  112 us
    unnamed x6, local copies, waits for them, and re-layouts  3.44 us

profile of v2, /device:TPU:0, one launch (start us, length us, event | category | flops | bytes accessed | tf_op | source)
XLA Modules:
  0.0 115.8 jit_solution(9454611750920525113)
XLA Ops:
  0.6 0.0 copy-start
  0.6 0.9 copy-done
  1.5 0.0 copy-start.1
  1.5 0.8 copy-done.1
  2.4 111.8 %shard_map.59 = (bf16[64,3968]{1,0:T(8,128)(2,1)S(1)}, bf16[64,7424]{1,0:T(8,128)(2,1)S(1)}) custom-call(bf16[8,3712]{1,0:T(8,128)(2,1)S(1)} %copy-done.1, s32[8,3712]{1,0:T(8,128)S(1)} %copy-done, bf16[3712,3968]{1,0:T(8,128)(2,1)} %qkv_ref.1, bf16[3712,7424]{1,0:T(8,128)(2,1)} %up_ref.1), custom_call_target="tpu_custom_call" | custom-call | flops 21650997248 | bytes 84574208 | tf_op jit(solution)/shard_map/pallas_call | solution.py:236
  114.1 0.8 copy.8
  114.9 0.9 copy.9
Async XLA Ops:
  0.6 0.9 copy-start
  1.5 0.8 copy-start.1

commit v3 on v2

--- a/solution.py
+++ b/solution.py
@@ -9,7 +9,8 @@
 
 KEEP_SCALE = 10.0 / 9.0
 WIDE = 256
-SLOTS = 3
+SLOTS = 8
+EARLY = 6
 LAG = 4
 MESH = pl.DeviceIdType.MESH
 
@@ -49,6 +50,9 @@
     mask_copy.start()
     first_tile = pltpu.make_async_copy(qkv_ref.at[:, pl.ds(0, head)], tiles.at[0, :, pl.ds(0, head)], tile_sem.at[0])
     first_tile.start()
+    for c in range(1, min(SLOTS, chunks)):
+        tile_copy(c, c)(lambda copy: copy.start())
+
     def peer(k):
         at = mine
         bit = 1
@@ -70,36 +74,30 @@
     def _():
         pl.semaphore_signal(barrier, inc=1, device_id={"kin": below}, device_id_type=MESH)
 
+    own_copy.wait()
     pl.semaphore_wait(barrier, peers - 1 + jnp.where(z < n - 1, 1, 0) + jnp.where(z > 0, 1, 0))
 
     def gather_copy(k):
         return pltpu.make_async_remote_copy(
-            src_ref=normed_ref, dst_ref=gathered.at[k],
+            src_ref=gathered.at[0], dst_ref=gathered.at[k],
             send_sem=gather_send.at[k - 1], recv_sem=gather_recv.at[k - 1],
             device_id={"nout": peer(k)}, device_id_type=MESH,
         )
 
     for k in range(peers - 1, 0, -1):
         gather_copy(k).start()
-    for c in range(1, min(SLOTS, chunks)):
-        tile_copy(c, c)(lambda copy: copy.start())
-
     mask_copy.wait()
-    keep = mask[...].astype(jnp.float32)
+    keep = mask[...].astype(jnp.float32) * KEEP_SCALE
     tokens = normed_ref.shape[0]
 
     def drop(x, source):
         x = x.astype(jnp.float32)
         for r in range(0, tokens, 2):
-            pair = [x[t : t + 1, :] * keep * KEEP_SCALE for t in (r, r + 1)]
+            pair = [x[t : t + 1, :] * keep for t in (r, r + 1)]
             row = pl.multiple_of((source * tokens + r) * passes, 2 * passes)
             dropped[pl.ds(row, 2 * passes), :] = jnp.concatenate(pair, axis=0).astype(jnp.bfloat16)
 
-    own_copy.wait()
     drop(gathered[0], mine)
-    for k in range(1, peers):
-        gather_copy(k).wait_recv()
-        drop(gathered[k], peer(k))
 
     def sized(c, body):
         @pl.when(c == 0)
@@ -128,20 +126,48 @@
 
     def compute(c, width):
         slot = lax.rem(c, SLOTS)
-        if width == WIDE and not isinstance(c, int):
-            tile_copy(c, slot)(lambda copy: copy.wait())
+        if not isinstance(c, int):
+            @pl.when(c >= EARLY)
+            def _():
+                tile_copy(c, slot)(lambda copy: copy.wait())
+
+        got = jnp.dot(dropped[...], tiles[slot, :, :width], preferred_element_type=jnp.float32)
+        own[c, :, :, :width] = got.reshape(n, block, width)
+
+        @pl.when(c + SLOTS < chunks)
+        def _():
+            tile_copy(c + SLOTS, slot)(lambda copy: copy.start())
+
+    for c in range(EARLY):
+        width = WIDE if c else head
+        if c:
+            tile_copy(c, c)(lambda copy: copy.wait())
         else:
             first_tile.wait()
-        got = jnp.dot(dropped[...], tiles[slot, :, :width], preferred_element_type=jnp.float32)
-        own[c, :, :, :width] = got.reshape(n, block, width)
-
-        @pl.when(c + SLOTS < chunks)
-        def _():
-            tile_copy(c + SLOTS, slot)(lambda copy: copy.start())
+
+        def send_early(buffer, copy_of):
+            rows = dropped[pl.ds(pl.multiple_of(mine * block, block), block), :]
+            part = jnp.dot(rows, tiles[c, :, :width], preferred_element_type=jnp.float32)
+            buffer[c, mine, :, :width] = part.astype(jnp.bfloat16)
+            copy_of(c, mine, width).start()
+
+        @pl.when((z == 0) & (mine > 0))
+        def _():
+            send_early(rising, rise_copy)
+
+        @pl.when((z == n - 1) & (mine < n - 1))
+        def _():
+            send_early(falling, fall_copy)
+
+    for k in range(1, peers):
+        gather_copy(k).wait_recv()
+        drop(gathered[k], peer(k))
 
     def forward(buffer, copy_of, at_end, d):
         def body(c, width):
-            @pl.when(at_end)
+            sent = at_end & (d == mine) & (c < EARLY)
+
+            @pl.when(at_end & jnp.logical_not(sent))
             def _():
                 buffer[c, d, :, :width] = own[c, d, :, :width].astype(jnp.bfloat16)
 
@@ -152,7 +178,9 @@
                     buffer[c, d, :, :width].astype(jnp.float32) + own[c, d, :, :width]
                 ).astype(jnp.bfloat16)
 
-            copy_of(c, d, width).start()
+            @pl.when(jnp.logical_not(sent))
+            def _():
+                copy_of(c, d, width).start()
         return body
 
     def finish(c, width):
@@ -232,7 +260,7 @@
     rows = tokens * peers * passes
     block = rows // n
     vmem = pl.BlockSpec(memory_space=pltpu.VMEM)
-    hbm = pl.BlockSpec(memory_space=pl.ANY)
+    hbm = pl.BlockSpec(memory_space=pltpu.HBM)
     qkv_out, up_out = pl.pallas_call(
         functools.partial(kernel, n, peers, passes, head, nq, chunks),
         out_shape=(
@@ -309,8 +337,10 @@
         and up_weight.shape[1] % WIDE == 0
         and tokens % 2 == 0
         and peers & (peers - 1) == 0
+        and peers == n
         and passes == 8
         and (tokens * peers * passes // n) % 16 == 0
+        and (qkv_weight.shape[1] + up_weight.shape[1]) // WIDE >= SLOTS
     )
     run = fused if aligned else plain
     return run(normed, keep_masks, qkv_weight, up_weight)

time: 116 us -> 115 us (level)
  no operation moved by 1% of the time
where the time goes in v3:
time: 115 us
  Pallas kernels  111 us (97%)
  local copies, waits for them, and re-layouts  3.44 us (3%)
    pallas_call x1, Pallas kernels, fused(): pl.pallas_call(functools.partial(kernel, n, peers, passes, head, nq, chun...  111 us
    unnamed x6, local copies, waits for them, and re-layouts  3.44 us

profile of v3, /device:TPU:0, one launch (start us, length us, event | category | flops | bytes accessed | tf_op | source)
XLA Modules:
  0.0 114.7 jit_solution(14101748306670411619)
XLA Ops:
  0.6 0.0 copy-start
  0.6 0.9 copy-done
  1.5 0.0 copy-start.1
  1.5 0.8 copy-done.1
  2.4 110.6 %shard_map.59 = (bf16[64,3968]{1,0:T(8,128)(2,1)S(1)}, bf16[64,7424]{1,0:T(8,128)(2,1)S(1)}) custom-call(bf16[8,3712]{1,0:T(8,128)(2,1)S(1)} %copy-done.1, s32[8,3712]{1,0:T(8,128)S(1)} %copy-done, bf16[3712,3968]{1,0:T(8,128)(2,1)} %qkv_ref.1, bf16[3712,7424]{1,0:T(8,128)(2,1)} %up_ref.1), custom_call_target="tpu_custom_call" | custom-call | flops 21650997248 | bytes 84574208 | tf_op jit(solution)/shard_map/pallas_call | solution.py:264
  113.0 0.8 copy.8
  113.8 0.9 copy.9
Async XLA Ops:
  0.6 0.9 copy-start
  1.5 0.8 copy-start.1

commit v4 on v3

--- a/solution.py
+++ b/solution.py
@@ -11,7 +11,7 @@
 WIDE = 256
 SLOTS = 8
 EARLY = 6
-LAG = 4
+LAG = 3
 MESH = pl.DeviceIdType.MESH
 
 

time: 115 us -> 115 us (level)
  no operation moved by 1% of the time
where the time goes in v4:
time: 115 us
  Pallas kernels  111 us (97%)
  local copies, waits for them, and re-layouts  3.44 us (3%)
    pallas_call x1, Pallas kernels, fused(): pl.pallas_call(functools.partial(kernel, n, peers, passes, head, nq, chun...  111 us
    unnamed x6, local copies, waits for them, and re-layouts  3.44 us

profile of v4, /device:TPU:0, one launch (start us, length us, event | category | flops | bytes accessed | tf_op | source)
XLA Modules:
  0.0 115.0 jit_solution(14893914687569477242)
XLA Ops:
  0.6 0.0 copy-start
  0.6 0.9 copy-done
  1.5 0.0 copy-start.1
  1.5 0.8 copy-done.1
  2.4 110.9 %shard_map.59 = (bf16[64,3968]{1,0:T(8,128)(2,1)S(1)}, bf16[64,7424]{1,0:T(8,128)(2,1)S(1)}) custom-call(bf16[8,3712]{1,0:T(8,128)(2,1)S(1)} %copy-done.1, s32[8,3712]{1,0:T(8,128)S(1)} %copy-done, bf16[3712,3968]{1,0:T(8,128)(2,1)} %qkv_ref.1, bf16[3712,7424]{1,0:T(8,128)(2,1)} %up_ref.1), custom_call_target="tpu_custom_call" | custom-call | flops 21650997248 | bytes 84574208 | tf_op jit(solution)/shard_map/pallas_call | solution.py:264
  113.3 0.8 copy.8
  114.1 0.9 copy.9
Async XLA Ops:
  0.6 0.9 copy-start
  1.5 0.8 copy-start.1
